TPU v7x, 512 devices: a whole 4x4x16 slice. The times are simulated.
512 devices in a mesh: group: 4 (over y_lo, core), fsdp: 8 (over x, y_hi), tensor: 16 (over z).
Axes of the slice: x: 4, y: 4 (y_hi: 2, y_lo: 2; y = y_hi * 2 + y_lo), z: 16, core: 2. Of those that a mesh axis runs over, the one named last changes fastest.
Arguments:
- tokens_in: bfloat16 [12288, 8192], P(('group', 'fsdp'), 'tensor'), may hold values from -6 to 6
- norm_gain: bfloat16 [8192], P('tensor'), may hold values from 0.099609375 to 1.8984375
- segment_ids: int32 [4, 3072], P('group'), may hold values from 0 to 3, never falling along the last dimension, each value on 1 to 1536 neighbouring positions
- wq: float32 [8192, 8192], P(('group', 'fsdp', 'tensor')), may hold values from -0.22097087 to 0.22097087
- wk: float32 [8192, 1024], P(('group', 'fsdp', 'tensor')), may hold values from -0.22097087 to 0.22097087
- wv: float32 [8192, 1024], P(('group', 'fsdp', 'tensor')), may hold values from -0.25 to 0.25
Outputs:
- attended: bfloat16 [12288, 8192], P(('group', 'fsdp'), 'tensor')
Inputs may be any that keep to these rules, and one draw needn't show every extreme that they name: segment_ids numbers the documents of each prompt, never falling along the prompt; each prompt holds 4 documents of 1 to 1536 tokens, one of exactly 1536.
All inputs are finite; a program needn't handle non-finite values.
Results may differ from a plain program's by a relative error of at most 0.012.
Values may be sent and summed in bfloat16 or wider, within the bound.
A program may use at most 64 MiB of HBM per device.

v0:
```python
import jax
import jax.numpy as jnp
from jax import lax
from jax.sharding import PartitionSpec as P

HD = 128


eps_norm = 1e-05
rope_base = 500000.0


def doc_positions(segments):
    positions = jnp.arange(segments.shape[0], dtype=jnp.int32)
    change = jnp.concatenate([jnp.ones((1,), dtype=bool), segments[1:] != segments[:-1]])
    begins = lax.cummax(jnp.where(change, positions, 0), axis=0)
    return positions - begins


def rotate(projected, places, heads):
    half_dim = HD // 2
    shaped = projected.reshape(projected.shape[0], heads, HD)
    inv_freq = jnp.power(rope_base, -jnp.arange(half_dim, dtype=jnp.float32) / half_dim)
    angles = places.astype(jnp.float32)[:, None] * inv_freq[None, :]
    cosine = jnp.cos(angles)[:, None, :]
    sine = jnp.sin(angles)[:, None, :]
    front_part = shaped[..., :half_dim]
    back_part = shaped[..., half_dim:]
    return jnp.concatenate(
        [front_part * cosine - back_part * sine, back_part * cosine + front_part * sine], axis=2
    )


def shards(tokens_in, norm_gain, segment_ids, wq, wk, wv):
    whole, gains = (
        lax.all_gather(tokens_in, "tensor", axis=1, tiled=True),
        lax.all_gather(norm_gain, "tensor", axis=0, tiled=True),
    )
    floats = whole.astype(jnp.float32)
    scale_rows = lax.rsqrt(jnp.mean(floats * floats, axis=1, keepdims=True) + eps_norm)
    normed = (floats * scale_rows * gains.astype(jnp.float32)).astype(jnp.bfloat16)
    tok_count = tokens_in.shape[0]
    row_count = wq.shape[0]
    q_source = wq.astype(jnp.bfloat16)
    key_heads = wk.astype(jnp.bfloat16).reshape(row_count, -1, HD)
    value_heads = wv.astype(jnp.bfloat16).reshape(row_count, -1, HD)
    paired = jnp.concatenate([key_heads, value_heads], axis=2)
    kv_source = jnp.repeat(paired, 2, axis=1).reshape(row_count, -1)
    q_columns, kv_columns = (
        lax.all_to_all(q_source, "tensor", split_axis=1, concat_axis=0, tiled=True),
        lax.all_to_all(kv_source, "tensor", split_axis=1, concat_axis=0, tiled=True),
    )
    q_proj = jnp.dot(
        normed,
        lax.all_gather(q_columns, ("group", "fsdp"), axis=0, tiled=True),
        preferred_element_type=jnp.float32,
    )
    kv_proj = jnp.dot(
        normed,
        lax.all_gather(kv_columns, ("group", "fsdp"), axis=0, tiled=True),
        preferred_element_type=jnp.float32,
    )
    k_proj = kv_proj[:, :HD]
    v_proj = kv_proj[:, HD:]
    segments = segment_ids[0]
    first_row = lax.axis_index("fsdp") * tok_count
    places = lax.dynamic_slice_in_dim(doc_positions(segments), first_row, tok_count)
    query_segments = lax.dynamic_slice_in_dim(segments, first_row, tok_count)
    head_count = q_proj.shape[1] // HD
    queries = rotate(q_proj, places, head_count).astype(jnp.bfloat16)
    keys_local = rotate(k_proj, places, 1).reshape(tok_count, HD).astype(jnp.bfloat16)
    values_local = v_proj.astype(jnp.bfloat16)
    keys_all, values_all = (
        lax.all_gather(keys_local, "fsdp", axis=0, tiled=True),
        lax.all_gather(values_local, "fsdp", axis=0, tiled=True),
    )
    query_index = first_row + jnp.arange(tok_count, dtype=jnp.int32)
    key_index = jnp.arange(keys_all.shape[0], dtype=jnp.int32)
    allowed = (key_index[None, :] <= query_index[:, None]) & (
        segments[None, :] == query_segments[:, None]
    )
    block_heads = head_count // 2
    block_count = head_count // block_heads
    stacked = queries.reshape(tok_count, block_count, block_heads, HD).transpose(1, 0, 2, 3)

    def attend_block(query_block):
        scores = jnp.einsum(
            "qhd,kd->hqk", query_block, keys_all, preferred_element_type=jnp.float32
        ) * HD ** (-0.5)
        masked = jnp.where(allowed[None], scores, -1e30)
        row_max = jnp.max(masked, axis=2, keepdims=True)
        exps = jnp.where(allowed[None], jnp.exp(masked - row_max), 0.0)
        attn_probs = (exps / jnp.sum(exps, axis=2, keepdims=True)).astype(jnp.bfloat16)
        mixed = jnp.einsum(
            "hqk,kd->qhd", attn_probs, values_all, preferred_element_type=jnp.float32
        )
        return mixed.astype(jnp.bfloat16)

    outputs = lax.map(attend_block, stacked)
    return outputs.transpose(1, 0, 2, 3).reshape(tok_count, head_count * HD)


def solution(mesh):
    placed = (
        P(("group", "fsdp"), "tensor"),
        P("tensor"),
        P("group", None),
        P(("group", "fsdp", "tensor"), None),
        P(("group", "fsdp", "tensor"), None),
        P(("group", "fsdp", "tensor"), None),
    )
    return jax.shard_map(
        shards,
        mesh=mesh,
        in_specs=placed,
        out_specs=P(("group", "fsdp"), "tensor"),
        check_vma=False,
    )
```

profile of v0, /device:TPU:49, one launch (start us, length us, event | category | flops | bytes accessed | tf_op | source)
XLA Modules:
  0.0 369.9 jit_solution(26759085626279335)
XLA Ops:
  6.5 0.7 all-gather.6.cloned.1.call-update
  7.3 0.8 convert_bitcast_fusion.1
  8.2 0.8 convert_bitcast_fusion
  9.1 26.4 %all_to_all.38 = bf16[16,16,256]{2,0,1:T(8,128)(2,1)} all-to-all(bf16[16,16,256]{2,0,1:T(8,128)(2,1)S(1)} %bitcast.99), channel_id=1, replica_groups=mesh['group'=4,'fsdp'=8,'tensor'=16] {'tensor'}, dimensions={1} | all-to-all | bytes 262144 | tf_op jit(solution)/shard_map/all_to_all | solution.py:51
  35.6 1.1 convert_element_type.41
  36.7 24.5 %all_to_all.39 = bf16[16,16,512]{2,0,1:T(8,128)(2,1)} all-to-all(bf16[16,16,512]{2,0,1:T(8,128)(2,1)S(1)} %bitcast.96), channel_id=1, replica_groups=mesh['group'=4,'fsdp'=8,'tensor'=16] {'tensor'}, dimensions={1} | all-to-all | bytes 524288 | tf_op jit(solution)/shard_map/all_to_all | solution.py:50
  61.3 0.7 reshape.170
  61.9 0.9 compare_reduce_fusion
  63.3 24.6 %all-gather.1 = bf16[16,1,512]{2,1,0:T(2,128)(2,1)S(1)} all-gather(bf16[1,1,512]{2,1,0:T(2,128)(2,1)S(1)} %reshape.170), channel_id=1, replica_groups=mesh['group'=4,'fsdp'=8,'tensor'=16] {'tensor'}, dimensions={0}, use_global_device_ids=true | all-gather | bytes 17408 | tf_op jit(solution)/shard_map/all_gather | solution.py:37
  88.0 0.7 dynamic-slice_reduce_fusion
  88.7 0.5 iota_add_fusion
  89.5 0.8 multiply_cosine_fusion
  90.3 18.2 %all-gather.6.cloned.1.call-done = bf16[384,8192]{1,0:T(8,128)(2,1)} async-done(((bf16[384,512]{1,0:T(8,128)(2,1)}), bf16[384,8192]{1,0:T(8,128)(2,1)}) %all-gather.6.cloned.1.call-update) | async-done | bytes 6291472 | tf_op jit(solution)/shard_map/all_gather | solution.py:36
  108.5 4.1 %fusion.40 = f32[384]{0:T(512)S(1)} fusion(bf16[384,8192]{1,0:T(8,128)(2,1)} %all-gather.6.cloned.1.call-done), kind=kLoop, calls=%fused_computation.33 | loop fusion | flops 9436800 | bytes 6292992 | tf_op jit(solution)/shard_map/reduce_sum | solution.py:40
  112.6 92.5 %all-gather.10.cloned.1.call-done = bf16[8192,256]{1,0:T(8,128)(2,1)} async-done(((bf16[256,256]{1,0:T(8,128)(2,1)}), bf16[8192,256]{1,0:T(8,128)(2,1)}) %all-gather.10.cloned.1.call-update) | async-done | bytes 4194320 | tf_op jit(solution)/shard_map/all_gather | solution.py:60
  205.1 6.6 %fusion.43 = f32[384,256]{0,1:T(8,128)S(1)} fusion(bf16[8192,256]{1,0:T(8,128)(2,1)} %all-gather.10.cloned.1.call-done, bf16[384,8192]{1,0:T(8,128)(2,1)} %all-gather.6.cloned.1.call-done, f32[8192]{0:T(1024)S(1)} %bitcast.103, f32[384]{0:T(512)S(1)} %add_rsqrt_fusion), kind=kOutput, calls=%fused_computation.36 | convolution fusion | flops 1623195648 | bytes 10913280 | tf_op jit(solution)/shard_map/dot_general | solution.py:58
  212.2 30.3 %all-gather = bf16[3072,1,128]{0,2,1:T(8,128)(2,1)S(1)} all-gather(bf16[384,1,128]{0,2,1:T(8,128)(2,1)S(1)} %pad_maximum_fusion), channel_id=2, replica_groups=mesh['group'=4,'fsdp'=8,'tensor'=16] {'fsdp'}, dimensions={0}, use_global_device_ids=true | all-gather | bytes 884736 | tf_op jit(solution)/shard_map/all_gather | solution.py:74
  242.9 30.6 %all_gather.23 = bf16[3072,128]{0,1:T(8,128)(2,1)S(1)} all-gather(bf16[384,128]{0,1:T(8,128)(2,1)S(1)} %slice.65), channel_id=1, replica_groups=mesh['group'=4,'fsdp'=8,'tensor'=16] {'fsdp'}, dimensions={0}, use_global_device_ids=true | all-gather | bytes 884736 | tf_op jit(solution)/shard_map/all_gather | solution.py:75
  273.9 47.8 %all-gather.8.cloned.1.call-done = bf16[8192,512]{1,0:T(8,128)(2,1)} async-done(((bf16[256,512]{1,0:T(8,128)(2,1)}), bf16[8192,512]{1,0:T(8,128)(2,1)}) %all-gather.8.cloned.1.call-update) | async-done | bytes 8388624 | tf_op jit(solution)/shard_map/all_gather | solution.py:55
  321.7 7.9 %fusion.45 = f32[384,512]{1,0:T(8,128)S(1)} fusion(bf16[8192,512]{1,0:T(8,128)(2,1)} %all-gather.8.cloned.1.call-done, bf16[384,8192]{1,0:T(8,128)(2,1)} %all-gather.6.cloned.1.call-done, f32[8192]{0:T(1024)} %bitcast.104, f32[384]{0:T(512)} %copy-done.4), kind=kOutput, calls=%fused_computation.37 | convolution fusion | flops 3233808384 | bytes 15500800 | tf_op jit(solution)/shard_map/dot_general | solution.py:53
  329.9 0.6 subtract_convert_fusion
  330.9 30.1 %while.11 = (s32[]{:T(128)}, bf16[2,384,2,128]{3,1,2,0:T(8,128)(2,1)}, bf16[2,384,2,128]{3,1,2,0:T(8,128)(2,1)S(1)}, bf16[3072,128]{1,0:T(8,128)(2,1)S(1)}, bf16...) while((s32[]{:T(128)}, ...), condition=%wide.region_6.7_spmd.clone, body=%wide.region_3.6_spmd.clone.sunk | while | flops 1228114944 | bytes 27546788 | solution.py:99
  330.9 2.0 fusion.76
  332.9 7.1 %fusion.77 = (f32[2,384]{1,0:T(2,128)}, f32[2,384,3072]{2,1,0:T(8,128)}) fusion(pred[384,3072]{1,0:T(8,128)(4,1)S(1)} %fusion.76, bf16[3072,128]{1,0:T(8,128)(2,1)S(1)} %get-tuple-element.189, bf16[2,384,2,128]{3,1,2,0:T(8,128)(2,1)S(1)} %get-tuple-element.188, s32[]{:T(128)S(6)} %copy.40), kind=kOutput, calls=%fused_computation.71.clone.1 | convolution fusion | flops 615779328 | bytes 12782596 | tf_op jit(solution)/shard_map/while/body/eval_jaxpr/sub | solution.py:92
  340.0 5.2 %fusion.78 = bf16[2,384,2,128]{3,1,2,0:T(8,128)(2,1)S(1)} fusion(bf16[2,384,2,128]{3,1,2,0:T(8,128)(2,1)S(1)} %copy-done.1, s32[]{:T(128)S(6)} %copy.40, f32[2,384,3072]{2,1,0:T(8,128)} %get-tuple-element.166, f32[2,384]{1,0:T(2,128)} %get-tuple-element.167, bf16[3072,128]{1,0:T(8,128)(2,1)S(1)} %get-tuple-element.190), kind=kOutput, calls=%fused_computation.17.clone.1 | convolution fusion | flops 608796672 | bytes 10423300 | tf_op jit(solution)/shard_map/while/body/eval_jaxpr/hqk,kd->qhd/dot_general | solution.py:94
  345.2 0.7 copy-done.2
  346.0 2.0 fusion.76
  348.0 7.1 %fusion.77 = (f32[2,384]{1,0:T(2,128)}, f32[2,384,3072]{2,1,0:T(8,128)}) fusion(pred[384,3072]{1,0:T(8,128)(4,1)S(1)} %fusion.76, bf16[3072,128]{1,0:T(8,128)(2,1)S(1)} %get-tuple-element.189, bf16[2,384,2,128]{3,1,2,0:T(8,128)(2,1)S(1)} %get-tuple-element.188, s32[]{:T(128)S(6)} %copy.40), kind=kOutput, calls=%fused_computation.71.clone.1 | convolution fusion | flops 615779328 | bytes 12782596 | tf_op jit(solution)/shard_map/while/body/eval_jaxpr/sub | solution.py:92
  355.1 5.2 %fusion.78 = bf16[2,384,2,128]{3,1,2,0:T(8,128)(2,1)S(1)} fusion(bf16[2,384,2,128]{3,1,2,0:T(8,128)(2,1)S(1)} %copy-done.1, s32[]{:T(128)S(6)} %copy.40, f32[2,384,3072]{2,1,0:T(8,128)} %get-tuple-element.166, f32[2,384]{1,0:T(2,128)} %get-tuple-element.167, bf16[3072,128]{1,0:T(8,128)(2,1)S(1)} %get-tuple-element.190), kind=kOutput, calls=%fused_computation.17.clone.1 | convolution fusion | flops 608796672 | bytes 10423300 | tf_op jit(solution)/shard_map/while/body/eval_jaxpr/hqk,kd->qhd/dot_general | solution.py:94
  360.3 0.7 copy-done.2
  361.0 1.4 copy.31
  362.4 0.9 reshape.168
  (44 shorter events, 2.9 us)
Async XLA Ops:
  6.5 101.9 %all-gather.6.cloned.1.call-start = ((), (), s32[]{:S(2)}) async-start(), calls=%async_computation.2 | async-start | bytes 6684672 | tf_op jit(solution)/shard_map/all_gather | solution.py:36
  7.3 197.8 %all-gather.10.cloned.1.call-start = ((), (), s32[]{:S(2)}) async-start(), calls=%async_computation.4 | async-start | bytes 4325376 | tf_op jit(solution)/shard_map/all_gather | solution.py:60
  35.5 286.2 %all-gather.8.cloned.1.call-start = ((), (), s32[]{:S(2)}) async-start(), calls=%async_computation.3 | async-start | bytes 8650752 | tf_op jit(solution)/shard_map/all_gather | solution.py:55
  88.0 123.7 %copy-start.3 = (f32[16,1,512]{2,1,0:T(1,128)}, f32[16,1,512]{2,1,0:T(1,128)S(1)}, u32[]{:S(2)}) copy-start(f32[16,1,512]{2,1,0:T(1,128)S(1)} %convert_element_type.46) | copy-start | bytes 98308
  112.6 99.1 %copy-start.4 = (f32[384]{0:T(512)}, f32[384]{0:T(512)S(1)}, u32[]{:S(2)}) copy-start(f32[384]{0:T(512)S(1)} %add_rsqrt_fusion) | copy-start | bytes 4612
  273.9 57.0 %copy-start = (s32[1,3072]{1,0:T(1,128)S(1)}, s32[1,3072]{1,0:T(1,128)}, u32[]{:S(2)}) copy-start(s32[1,3072]{1,0:T(1,128)} %param.10) | copy-start | bytes 36868
  332.9 7.1 %copy-start.1 = (bf16[2,384,2,128]{3,1,2,0:T(8,128)(2,1)S(1)}, bf16[2,384,2,128]{3,1,2,0:T(8,128)(2,1)}, u32[]{:S(2)}) copy-start(bf16[2,384,2,128]{3,1,2,0:T(8,128)(2,1)} %get-tuple-element.178) | copy-start | bytes 1179652 | tf_op jit(solution)/shard_map/while
  345.2 0.7 copy-start.2
  348.0 7.1 %copy-start.1 = (bf16[2,384,2,128]{3,1,2,0:T(8,128)(2,1)S(1)}, bf16[2,384,2,128]{3,1,2,0:T(8,128)(2,1)}, u32[]{:S(2)}) copy-start(bf16[2,384,2,128]{3,1,2,0:T(8,128)(2,1)} %get-tuple-element.178) | copy-start | bytes 1179652 | tf_op jit(solution)/shard_map/while
  360.3 0.7 copy-start.2
Sparse Core Ops, SparseCore 0:
  9.4 98.9 all-gather.5
  110.6 94.4 all-gather.9
  207.2 114.5 all-gather.7
where the time goes:
time: 370 us
  waiting for transfers between devices  159 us (43%)
  blocking collectives  136 us (37%)
  matrix products  39.1 us (11%)
  other arithmetic  15 us (4%)
  between operations  13.3 us (4%)
  local copies, waits for them, and re-layouts  6.65 us (2%)
    all_gather x1, waiting for transfers between devices, shards(): lax.all_gather(kv_columns, ('group', 'fsdp'), axis=0, tiled=True)  92.5 us
    all_gather x1, waiting for transfers between devices, shards(): lax.all_gather(q_columns, ('group', 'fsdp'), axis=0, tiled=True)  47.8 us
    all_gather x1, blocking collectives, shards(): lax.all_gather(values_local, 'fsdp', axis=0, tiled=True)  30.6 us
    all_gather x1, blocking collectives, shards(): lax.all_gather(keys_local, 'fsdp', axis=0, tiled=True)  30.3 us
    all_to_all x1, blocking collectives, shards(): lax.all_to_all(kv_source, 'tensor', split_axis=1, concat_axis=0, tiled=True)  26.4 us
    all_gather x1, blocking collectives, shards(): lax.all_gather(norm_gain, 'tensor', axis=0, tiled=True)  24.6 us
    all_to_all x1, blocking collectives, shards(): lax.all_to_all(q_source, 'tensor', split_axis=1, concat_axis=0, tiled=True)  24.5 us
    all_gather x1, waiting for transfers between devices, shards(): lax.all_gather(tokens_in, 'tensor', axis=1, tiled=True)  18.2 us
  transfers between devices with their start and end apart: 3, of which 3 were waited for; matrix products, arithmetic and copies ran while one was open for 5% of the time, Pallas kernels for 0%

commit v1 on v0

v1 whole, which is shorter than its diff:
```python
import functools

import jax
import jax.numpy as jnp
import numpy as np
from jax import lax
from jax.experimental import pallas as pl
from jax.experimental.pallas import tpu as pltpu
from jax.sharding import PartitionSpec as P

MESH = pl.DeviceIdType.MESH
F32, BF16 = jnp.float32, jnp.bfloat16
HD = 128
ROWS = 384
FEAT = 512
NZ = 16
CHUNKS, CHUNK = 3, 128
HALF = CHUNK // 2
COLS = 640
BACK = 4
BAND = (BACK + 1) * ROWS
EPS = 1e-05
T_PLANE1, T_PLANE2, T_PLANE3, T_MM = 1, 5, 11, 12


def document_starts(seg):
    return [jnp.sum(jnp.where(seg < d, 1.0, 0.0), axis=1, keepdims=True) for d in (1, 2, 3)]


def start_of(row, begins):
    start = jnp.zeros_like(row)
    for b in begins:
        start = jnp.where(row >= b, b, start)
    return start


def front(tok_ref, gain_ref, seg_ref, freq_ref, wq_ref, wk_ref, wv_ref, q_ref, k_ref, v_ref,
          wsend, wbuf, tok, ssq, acc, trig, kv,
          a_send, a_recv, s_send, s_recv, p_send, p_recv, b_send, b_recv, r_send, r_recv, k_send, k_recv):
    g, f, z = lax.axis_index("group"), lax.axis_index("fsdp"), lax.axis_index("tensor")
    x, y, c = f // 2, (f % 2) * 2 + g // 2, g % 2
    par = z % 2
    mate = z + 1 - 2 * par

    def chip(px, py, core):
        return (py % 2) * 2 + core, px * 2 + py // 2

    def place(first, second, core=None):
        return chip((x + (1 - c) * first + c * second) % 4, (y + c * first + (1 - c) * second) % 4, c)

    def dev(gf, zz):
        return {"group": gf[0], "fsdp": gf[1], "tensor": zz}

    def copy(src, dst, send, recv, to):
        return pltpu.make_async_remote_copy(src_ref=src, dst_ref=dst, send_sem=send, recv_sem=recv, device_id=to, device_id_type=MESH)

    bar = pltpu.get_barrier_semaphore()
    count = 0
    for d in range(1, NZ):
        pl.semaphore_signal(bar, inc=1, device_id=dev((g, f), (z + d) % NZ), device_id_type=MESH)
        count += 1
    for d in (1, 2, 3):
        for to in (place(d, 0), place(0, d)):
            pl.semaphore_signal(bar, inc=1, device_id=dev(to, z), device_id_type=MESH)
            count += 1
    sibling = chip(x, y, 1 - c)
    pl.semaphore_signal(bar, inc=1, device_id=dev(sibling, z), device_id_type=MESH)
    count += 1
    for d in range(1, 8):
        for zz in (z, mate):
            pl.semaphore_signal(bar, inc=1, device_id=dev((g, (f + d) % 8), zz), device_id_type=MESH)
            count += 1

    floats = tok_ref[...].astype(F32)
    part = jnp.sum(floats * floats, axis=1, keepdims=True)
    ssq[z] = jnp.broadcast_to(part, (ROWS, 128)).T[0:1]

    for d in range(NZ):
        wsend[d, :, 0:512] = wq_ref[:, 512 * d:512 * d + 512].astype(BF16)
        side = (wk_ref, wv_ref)[d % 2]
        wsend[d, :, 512:640] = side[:, 128 * (d // 2):128 * (d // 2) + 128].astype(BF16)
    slot = g * 8 + f
    my_rows = pl.ds(pl.multiple_of(z * 16, 16), 16)

    pl.semaphore_wait(bar, count)

    def square(d):
        to = (z + d) % NZ
        return copy(ssq.at[z], ssq.at[z], s_send.at[d], s_recv.at[d], dev((g, f), to))

    def relay(d):
        to = (z + d) % NZ
        return copy(wsend.at[to], wbuf.at[slot, my_rows], a_send.at[d], a_recv.at[d], dev((g, f), to))

    for d in range(1, NZ):
        square(d).start()
    for d in range(1, NZ):
        relay(d).start()
    wbuf[slot, my_rows, :] = wsend[z]

    for d in range(1, BACK + 1):
        @pl.when(f < d)
        def _():
            kv[:, (BACK - d) * ROWS:(BACK - d + 1) * ROWS, :] = jnp.zeros((2, ROWS, HD), BF16)

    begins = document_starts(seg_ref[...])
    row = (lax.broadcasted_iota(jnp.int32, (ROWS, HD), 0) + f * ROWS).astype(F32)
    angle = (row - start_of(row, begins)) * freq_ref[...]
    cosine, sine = jnp.cos(angle), jnp.sin(angle)
    lane = lax.broadcasted_iota(jnp.int32, (ROWS, HD), 1)
    trig[0] = cosine
    trig[1] = jnp.where(lane < HD // 2, -sine, sine)

    for d in range(1, NZ):
        square(d).wait_recv()
    total = jnp.sum(ssq[...], axis=0)
    scale = lax.rsqrt(jnp.broadcast_to(total, (128, ROWS)).T * (1.0 / 8192) + EPS)
    for j in range(FEAT // 128):
        cut = slice(128 * j, 128 * j + 128)
        tok[z, :, cut] = (tok_ref[:, cut].astype(F32) * scale * gain_ref[:, cut].astype(F32)).astype(BF16)

    def hop(ch, step, h, r):
        to = (z + 1 - 2 * r + NZ) % NZ
        owner = (z + NZ + (2 * r - 1) * step) % NZ
        ref = tok.at[owner, pl.ds(pl.multiple_of(ch * CHUNK + h * HALF, HALF), HALF)]
        i = (ch * 8 + step) * 2 + h
        return copy(ref, ref, r_send.at[r, i], r_recv.at[r, i], dev((g, f), to))

    WAYS = ((0, 0), (0, 1), (1, 0), (1, 1))

    def is_long(h, r):
        return h == r

    def ring(ch, step, h):
        for r in (0, 1):
            @pl.when(step > 0)
            def _():
                hop(ch, step - 1, h, r).wait_recv()
            if is_long(h, r):
                hop(ch, step, h, r).start()
            else:
                @pl.when(step < 7)
                def _():
                    hop(ch, step, h, r).start()

    def last_arrivals(ch):
        for h in (0, 1):
            hop(ch, 7, h, h).wait_recv()

    def slot_at(first, second):
        gf = place(first, second)
        return gf[0] * 8 + gf[1]

    def to_first(d):
        ref = wbuf.at[slot]
        return copy(ref, ref, p_send.at[d - 1], p_recv.at[d - 1], dev(place(d, 0), z))

    def to_second(j, d):
        ref = wbuf.at[slot_at(j, 0)]
        i = 3 + j * 3 + d - 1
        return copy(ref, ref, p_send.at[i], p_recv.at[i], dev(place(0, d), z))

    def to_sibling(j, d):
        ref = wbuf.at[slot_at(j, d)]
        i = j * 4 + d
        return copy(ref, ref, b_send.at[i], b_recv.at[i], dev(sibling, z))

    def plane1():
        for d in range(1, NZ):
            relay(d).wait_recv()
        for d in (1, 3, 2):
            to_first(d).start()
        for d in (1, 3, 2):
            to_second(0, d).start()
        to_sibling(0, 0).start()

    def plane2():
        for d in (1, 3, 2):
            to_first(d).wait_recv()
            for e in (1, 3, 2):
                to_second(4 - d, e).start()
            to_sibling(4 - d, 0).start()

    def plane3():
        for j in range(4):
            for d in (1, 3, 2):
                to_second(j, d).wait_recv()
                to_sibling(j, 4 - d).start()
        for j in range(4):
            for d in range(4):
                to_sibling(j, d).wait_recv()

    def multiply(ch, offset, first):
        owner = (z + offset + NZ) % NZ
        rows = pl.ds(pl.multiple_of(ch * CHUNK, CHUNK), CHUNK)
        w = wbuf[pl.ds(owner * 2, 2)].reshape(FEAT, COLS)
        prod = jnp.dot(tok[owner, rows, :], w, preferred_element_type=F32)
        if first:
            acc[rows, :] = prod
        else:
            acc[rows, :] += prod

    def kv_copy(ch, d, other):
        src = kv.at[par, pl.ds(pl.multiple_of(BACK * ROWS + ch * CHUNK, CHUNK), CHUNK)]
        dst = kv.at[par, pl.ds(pl.multiple_of((BACK - d) * ROWS + ch * CHUNK, CHUNK), CHUNK)]
        i = ch * 5 + d
        zz = mate if other else z
        return copy(src, dst, k_send.at[int(other), i], k_recv.at[par, i], dev((g, (f + d) % 8), zz))

    def finish(ch):
        rows = pl.ds(pl.multiple_of(ch * CHUNK, CHUNK), CHUNK)
        cosine, sine = trig[0, rows, :], trig[1, rows, :]
        for h in range(4):
            a = acc[rows, HD * h:HD * h + HD]
            q_ref[rows, HD * h:HD * h + HD] = (a * cosine + pltpu.roll(a, HD // 2, 1) * sine).astype(BF16)
        a = acc[rows, 512:640]
        is_key = par == 0
        rotated = jnp.where(is_key, a * cosine + pltpu.roll(a, HD // 2, 1) * sine, a)
        kv[par, pl.ds(pl.multiple_of(BACK * ROWS + ch * CHUNK, CHUNK), CHUNK), :] = rotated.astype(BF16)
        kv_copy(ch, 0, True).start()
        for d in (4, 3, 2, 1):
            @pl.when(f + d < 8)
            def _():
                kv_copy(ch, d, False).start()
                kv_copy(ch, d, True).start()

    def slot_step(t, _):
        ch, step = t // 8, t % 8
        m = t - T_MM
        mch, quarter = m // 4, m % 4

        def some(n):
            i = quarter * 4 + n
            multiply(mch, (i + 1) // 2 * (2 * (i % 2) - 1), False)

        ring(ch, step, 0)

        @pl.when((t >= T_MM) & (quarter == 0))
        def _():
            rows = pl.ds(pl.multiple_of(mch * CHUNK, CHUNK), CHUNK)
            acc[rows, :] = jnp.zeros((CHUNK, COLS), F32)

        @pl.when(t >= T_MM)
        def _():
            some(0)

        ring(ch, step, 1)

        @pl.when(t >= T_MM)
        def _():
            some(1)
            some(2)

            @pl.when(t < CHUNKS * 8 - 1)
            def _():
                some(3)

        @pl.when(t == T_PLANE1)
        def _():
            plane1()

        @pl.when(t == T_PLANE2)
        def _():
            plane2()

        @pl.when(t == T_PLANE3)
        def _():
            plane3()

        @pl.when((step == 1) & (ch > 0))
        def _():
            last_arrivals(ch - 1)

        @pl.when((t >= T_MM) & (quarter == 3) & (mch < CHUNKS - 1))
        def _():
            finish(mch)
        return 0

    lax.fori_loop(0, CHUNKS * 8, slot_step, 0)
    last_arrivals(CHUNKS - 1)
    multiply(CHUNKS - 1, 8, False)
    finish(CHUNKS - 1)

    def kv_wait(kind, ch, d):
        dst = kv.at[kind, pl.ds((BACK - d) * ROWS + ch * CHUNK, CHUNK)]
        i = ch * 5 + d
        copy(dst, dst, k_send.at[0, i], k_recv.at[kind, i], dev((g, f), z)).wait_recv()

    for ch in range(CHUNKS):
        kv_wait(1 - par, ch, 0)
        for d in range(1, BACK + 1):
            @pl.when(f >= d)
            def _():
                kv_wait(0, ch, d)
                kv_wait(1, ch, d)
    k_ref[...] = kv[0]
    v_ref[...] = kv[1]

    for d in range(1, NZ):
        square(d).wait_send()
        relay(d).wait_send()
    for d in (1, 2, 3):
        to_first(d).wait_send()
    for j in range(4):
        for d in (1, 2, 3):
            to_second(j, d).wait_send()
        for d in range(4):
            to_sibling(j, d).wait_send()

    def drain(t, _):
        ch, step = t // 8, t % 8
        for h, r in WAYS:
            if is_long(h, r):
                hop(ch, step, h, r).wait_send()
            else:
                @pl.when(step < 7)
                def _():
                    hop(ch, step, h, r).wait_send()
        return 0

    lax.fori_loop(0, CHUNKS * 8, drain, 0)
    for ch in range(CHUNKS):
        kv_copy(ch, 0, True).wait_send()
        for d in (4, 3, 2, 1):
            @pl.when(f + d < 8)
            def _():
                kv_copy(ch, d, False).wait_send()
                kv_copy(ch, d, True).wait_send()


def attend(q_ref, k_ref, v_ref, seg_ref, o_ref, bias):
    f = lax.axis_index("fsdp")
    begins = document_starts(seg_ref[...])
    width = BACK * ROWS + CHUNK
    for i in range(CHUNKS):
        rows = slice(i * CHUNK, (i + 1) * CHUNK)
        keys = slice(i * CHUNK, i * CHUNK + width)
        q_at = (lax.broadcasted_iota(jnp.int32, (CHUNK, 128), 0) + (f * ROWS + i * CHUNK)).astype(F32)
        start = start_of(q_at, begins)
        for j in range(width // 128):
            k_at = (lax.broadcasted_iota(jnp.int32, (CHUNK, 128), 1) + ((f - BACK) * ROWS + i * CHUNK + j * 128)).astype(F32)
            bias[:, 128 * j:128 * j + 128] = jnp.where((k_at >= start) & (k_at <= q_at), 0.0, -1e30)
        for h in range(4):
            cols = slice(HD * h, HD * h + HD)
            s = lax.dot_general(q_ref[rows, cols], k_ref[keys, :], (((1,), (1,)), ((), ())), preferred_element_type=F32)
            s = s * HD ** (-0.5) + bias[...]
            p = jnp.exp(s - jnp.max(s, axis=1, keepdims=True))
            total = jnp.sum(p, axis=1, keepdims=True)
            o = jnp.dot(p.astype(BF16), v_ref[keys, :], preferred_element_type=F32)
            o_ref[rows, cols] = (o / total).astype(BF16)


def shards(tokens_in, norm_gain, segment_ids, wq, wk, wv):
    vmem = pl.BlockSpec(memory_space=pltpu.VMEM)
    dma = pltpu.SemaphoreType.DMA
    freqs = 500000.0 ** (-(np.arange(HD) % 64) / 64.0)
    q, k, v = pl.pallas_call(
        front,
        name="front",
        out_shape=[
            jax.ShapeDtypeStruct((ROWS, 512), BF16),
            jax.ShapeDtypeStruct((BAND, HD), BF16),
            jax.ShapeDtypeStruct((BAND, HD), BF16),
        ],
        in_specs=[vmem] * 7,
        out_specs=[vmem] * 3,
        scratch_shapes=[
            pltpu.VMEM((NZ, 16, COLS), BF16),
            pltpu.VMEM((32, 256, COLS), BF16),
            pltpu.VMEM((NZ, ROWS, FEAT), BF16),
            pltpu.VMEM((NZ, 1, ROWS), F32),
            pltpu.VMEM((ROWS, COLS), F32),
            pltpu.VMEM((2, ROWS, HD), F32),
            pltpu.VMEM((2, BAND, HD), BF16),
            dma((NZ,)), dma((NZ,)),
            dma((NZ,)), dma((NZ,)),
            dma((15,)), dma((15,)),
            dma((16,)), dma((16,)),
            dma((2, CHUNKS * 16)), dma((2, CHUNKS * 16)),
            dma((2, CHUNKS * 5)), dma((2, CHUNKS * 5)),
        ],
        compiler_params=pltpu.CompilerParams(collective_id=1, has_side_effects=True, vmem_limit_bytes=48 << 20),
        cost_estimate=pl.CostEstimate(flops=2 * ROWS * 8192 * COLS, bytes_accessed=4 << 20, transcendentals=0),
    )(tokens_in, norm_gain[None], segment_ids, jnp.asarray(freqs[None], F32), wq, wk, wv)
    return pl.pallas_call(
        attend,
        name="attend",
        out_shape=jax.ShapeDtypeStruct((ROWS, 512), BF16),
        in_specs=[vmem] * 4,
        out_specs=vmem,
        scratch_shapes=[pltpu.VMEM((CHUNK, BACK * ROWS + CHUNK), F32)],
        compiler_params=pltpu.CompilerParams(vmem_limit_bytes=32 << 20),
        cost_estimate=pl.CostEstimate(flops=4 * 4 * ROWS * 1664 * HD, bytes_accessed=4 << 20, transcendentals=4 * ROWS * 1664),
    )(q, k, v, segment_ids)


def solution(mesh):
    placed = (
        P(("group", "fsdp"), "tensor"),
        P("tensor"),
        P("group", None),
        P(("group", "fsdp", "tensor"), None),
        P(("group", "fsdp", "tensor"), None),
        P(("group", "fsdp", "tensor"), None),
    )
    return jax.shard_map(
        shards,
        mesh=mesh,
        in_specs=placed,
        out_specs=P(("group", "fsdp"), "tensor"),
        check_vma=False,
    )
```

time: 370 us -> 151 us (0.41)
  the two profiles are of different devices: /device:TPU:49 before, /device:TPU:2 now
where the time goes in v1:
time: 151 us
  Pallas kernels  146 us (97%)
  local copies, waits for them, and re-layouts  5.12 us (3%)
    pallas_call x1, Pallas kernels, shards(): pl.pallas_call(front, name='front', out_shape=[jax.ShapeDtypeStruct((ROWS...  139 us
    pallas_call x1, Pallas kernels, shards(): pl.pallas_call(attend, name='attend', out_shape=jax.ShapeDtypeStruct((ROW...  6.9 us
    unnamed x12, local copies, waits for them, and re-layouts  4.42 us

profile of v1, /device:TPU:2, one launch (start us, length us, event | category | flops | bytes accessed | tf_op | source)
XLA Modules:
  0.0 151.0 jit_solution(17073050867417396494)
XLA Ops:
  0.0 0.0 copy-start.5
  0.0 0.7 broadcast_in_dim.3.gain_ref
  0.7 0.0 copy-done.5
  0.7 0.0 copy-start
  0.7 1.0 copy-done
  1.7 0.0 copy-start.1
  1.7 1.0 copy-done.1
  2.7 0.0 copy-start.2
  2.7 0.8 copy-done.2
  3.6 0.0 copy-start.3
  3.6 0.8 copy-done.3
  4.4 0.0 copy-start.4
  4.4 0.7 copy-done.4
  5.1 139.0 %front.1 = (bf16[384,512]{1,0:T(8,128)(2,1)S(1)}, bf16[1920,128]{1,0:T(8,128)(2,1)S(1)}, bf16[1920,128]{1,0:T(8,128)(2,1)S(1)}) custom-call(bf16[384,512]{1,0:T(8,128)(2,1)S(1)} %copy-done.1, bf16[1,512]{1,0:T(2,128)(2,1)S(1)} %broadcast_in_dim.3.gain_ref, s32[1,3072]{1,0:T(1,128)S(1)} %copy-done.4, f32[1,128]{1,0:T(1,128)S(1)} %copy-done.5, ...), custom_call_target="tpu_custom_call" | custom-call | flops 4026531840 | bytes 4194304 | tf_op jit(solution)/shard_map/front/pallas_call | solution.py:357
  144.1 6.9 %attend.1 = bf16[384,512]{1,0:T(8,128)(2,1)} custom-call(bf16[384,512]{1,0:T(8,128)(2,1)S(1)} %get-tuple-element.8.q_ref, bf16[1920,128]{1,0:T(8,128)(2,1)S(1)} %get-tuple-element.9.k_ref, bf16[1920,128]{1,0:T(8,128)(2,1)S(1)} %get-tuple-element.10.v_ref, s32[1,3072]{1,0:T(1,128)S(1)} %copy-done.4), custom_call_target="tpu_custom_call" | custom-call | flops 1308622848 | bytes 4194304 | tf_op jit(solution)/shard_map/attend/pallas_call | solution.py:385
Async XLA Ops:
  0.0 0.7 copy-start.5
  0.7 1.0 copy-start
  1.7 1.0 copy-start.1
  2.7 0.8 copy-start.2
  3.6 0.8 copy-start.3
  4.4 0.7 copy-start.4

commit v2 on v1

v2 whole, which is shorter than its diff:
```python
import math

import jax
import jax.numpy as jnp
import numpy as np
from jax import lax
from jax.experimental import pallas as pl
from jax.experimental.pallas import tpu as pltpu
from jax.sharding import PartitionSpec as P

MESH = pl.DeviceIdType.MESH
F32, BF16 = jnp.float32, jnp.bfloat16
HD = 128
ROWS = 384
FEAT = 512
NZ = 16
SIZES = (192, 128, 64)
CHUNKS = len(SIZES)
FROM = (0, 192, 320)
LAG = 2
COLS = 768
BACK = 4
LOG2E = math.log2(math.e)
EPS = 1e-05


def document_starts(seg):
    return [jnp.sum(jnp.where(seg < d, 1.0, 0.0), axis=1, keepdims=True) for d in (1, 2, 3)]


def start_of(row, begins):
    start = jnp.zeros_like(row)
    for b in begins:
        start = jnp.where(row >= b, b, start)
    return start


def key_rows(ch, d):
    return pl.ds((BACK + 1) * FROM[ch] + (BACK - d) * SIZES[ch], SIZES[ch])


def front(tok_hbm, gain_ref, seg_hbm, freq_hbm, wq_hbm, wk_hbm, wv_hbm, o_ref,
          tok_ref, seg_ref, freq_ref, wq_ref, wk_ref, wv_ref,
          wsend, wbuf, tok, ssq, acc, trig, kv, queries, *rest):
    bias = rest[:CHUNKS]
    (peak, mixed, in_sem,
          a_send, a_recv, s_send, s_recv, p_send, p_recv, b_send, b_recv, r_send, r_recv, k_send, k_recv) = rest[CHUNKS:]
    g, f, z = lax.axis_index("group"), lax.axis_index("fsdp"), lax.axis_index("tensor")
    x, y, c = f // 2, (f % 2) * 2 + g // 2, g % 2

    def chip(px, py, core):
        return (py % 2) * 2 + core, px * 2 + py // 2

    def place(first, second, core=None):
        return chip((x + (1 - c) * first + c * second) % 4, (y + c * first + (1 - c) * second) % 4, c)

    def dev(gf, zz):
        return {"group": gf[0], "fsdp": gf[1], "tensor": zz}

    def copy(src, dst, send, recv, to):
        return pltpu.make_async_remote_copy(src_ref=src, dst_ref=dst, send_sem=send, recv_sem=recv, device_id=to, device_id_type=MESH)

    loads = [
        pltpu.make_async_copy(src, dst, in_sem.at[i])
        for i, (src, dst) in enumerate((
            (tok_hbm, tok_ref), (wq_hbm, wq_ref), (wk_hbm, wk_ref), (wv_hbm, wv_ref),
            (seg_hbm, seg_ref), (freq_hbm, freq_ref)))
    ]
    for load in loads:
        load.start()

    bar = pltpu.get_barrier_semaphore()
    count = 0
    for d in range(1, NZ):
        pl.semaphore_signal(bar, inc=1, device_id=dev((g, f), (z + d) % NZ), device_id_type=MESH)
        count += 1
    for d in (1, 3):
        for to in (place(d, 0), place(0, d)):
            pl.semaphore_signal(bar, inc=1, device_id=dev(to, z), device_id_type=MESH)
            count += 1
    sibling = chip(x, y, 1 - c)
    pl.semaphore_signal(bar, inc=1, device_id=dev(sibling, z), device_id_type=MESH)
    count += 1
    for d in range(1, 8):
        pl.semaphore_signal(bar, inc=1, device_id=dev((g, (f + d) % 8), z), device_id_type=MESH)
        count += 1

    loads[0].wait()
    floats = tok_ref[...].astype(F32)
    part = jnp.sum(floats * floats, axis=1, keepdims=True)
    ssq[z] = jnp.broadcast_to(part, (ROWS, 128)).T[0:1]

    for load in loads[1:4]:
        load.wait()
    for d in range(NZ):
        wsend[d, :, 0:512] = wq_ref[:, 512 * d:512 * d + 512].astype(BF16)
        head = slice(HD * (d // 2), HD * (d // 2) + HD)
        wsend[d, :, 512:640] = wk_ref[:, head].astype(BF16)
        wsend[d, :, 640:768] = wv_ref[:, head].astype(BF16)
    slot = g * 8 + f
    my_rows = pl.ds(pl.multiple_of(z * 16, 16), 16)

    pl.semaphore_wait(bar, count)

    def square(d):
        to = (z + d) % NZ
        return copy(ssq.at[z], ssq.at[z], s_send.at[d], s_recv.at[d], dev((g, f), to))

    def relay(d):
        to = (z + d) % NZ
        return copy(wsend.at[to], wbuf.at[slot, my_rows], a_send.at[d], a_recv.at[d], dev((g, f), to))

    for d in range(1, NZ):
        square(d).start()
    for d in range(1, NZ):
        relay(d).start()
    wbuf[slot, my_rows, :] = wsend[z]

    kv[:, 256:384] = jnp.ones(((BACK + 1) * ROWS, HD), BF16)
    for d in range(1, BACK + 1):
        @pl.when(f < d)
        def _():
            for ch in range(CHUNKS):
                kv[key_rows(ch, d), 0:256] = jnp.zeros((SIZES[ch], 256), BF16)

    for load in loads[4:]:
        load.wait()
    begins = document_starts(seg_ref[...])
    row = (lax.broadcasted_iota(jnp.int32, (ROWS, HD), 0) + f * ROWS).astype(F32)
    start = start_of(row, begins)
    angle = (row - start) * freq_ref[...]
    cosine, sine = jnp.cos(angle), jnp.sin(angle)
    lane = lax.broadcasted_iota(jnp.int32, (ROWS, HD), 1)
    trig[0] = cosine
    trig[1] = jnp.where(lane < HD // 2, -sine, sine)

    for d in range(1, NZ):
        square(d).wait_recv()
    total = jnp.sum(ssq[...], axis=0)
    scale = lax.rsqrt(jnp.broadcast_to(total, (128, ROWS)).T * (1.0 / 8192) + EPS)
    for j in range(FEAT // 128):
        cut = slice(128 * j, 128 * j + 128)
        tok[z, :, cut] = (tok_ref[:, cut].astype(F32) * scale * gain_ref[:, cut].astype(F32)).astype(BF16)

    def hop(ch, step, h, r):
        to = (z + 1 - 2 * r + NZ) % NZ
        owner = (z + NZ + (2 * r - 1) * step) % NZ
        ref = tok.at[owner, pl.ds(FROM[ch] + h * SIZES[ch] // 2, SIZES[ch] // 2)]
        i = (ch * 8 + step) * 2 + h
        return copy(ref, ref, r_send.at[r, i], r_recv.at[r, i], dev((g, f), to))

    WAYS = ((0, 0), (0, 1), (1, 0), (1, 1))

    def is_long(h, r):
        return h == r

    def ring(ch, step, h):
        for r in (0, 1):
            if step > 0:
                hop(ch, step - 1, h, r).wait_recv()
            if is_long(h, r) or step < 7:
                hop(ch, step, h, r).start()

    def last_arrivals(ch):
        for h in (0, 1):
            hop(ch, 7, h, h).wait_recv()

    def slot_at(first, second):
        gf = place(first, second)
        return gf[0] * 8 + gf[1]

    def ring4_ref(k, pos):
        return wbuf.at[slot_at(pos, 0) if k == 0 else slot_at(k - 1, pos)]

    def ring4_place(k, d):
        return place(d, 0) if k == 0 else place(0, d)

    def near(k, d):
        ref = ring4_ref(k, 0)
        i = k * 4 + d // 2
        return copy(ref, ref, p_send.at[i], p_recv.at[i], dev(ring4_place(k, d), z))

    def far(k, d):
        ref = ring4_ref(k, 4 - d).at[pl.ds((d // 2) * 128, 128)]
        i = k * 4 + 2 + d // 2
        return copy(ref, ref, p_send.at[i], p_recv.at[i], dev(ring4_place(k, d), z))

    def to_sibling(j, d):
        ref = wbuf.at[slot_at(j, d)]
        i = j * 4 + d
        return copy(ref, ref, b_send.at[i], b_recv.at[i], dev(sibling, z))

    def start_ring4(k):
        near(k, 1).start()
        near(k, 3).start()

    def forward_ring4(k):
        for d in (1, 3):
            near(k, d).wait_recv()
            far(k, d).start()

    def end_ring4(k):
        for d in (1, 3):
            far(k, d).wait_recv()

    def plane1():
        for d in range(1, NZ):
            relay(d).wait_recv()
        start_ring4(0)
        start_ring4(1)
        to_sibling(0, 0).start()

    def plane2():
        forward_ring4(0)
        start_ring4(4)
        start_ring4(2)
        to_sibling(3, 0).start()
        to_sibling(1, 0).start()

    def plane3():
        end_ring4(0)
        start_ring4(3)
        to_sibling(2, 0).start()
        forward_ring4(1)
        to_sibling(0, 3).start()
        to_sibling(0, 1).start()

    def plane4():
        for k in (4, 2):
            forward_ring4(k)
            to_sibling(k - 1, 3).start()
            to_sibling(k - 1, 1).start()
        end_ring4(1)
        to_sibling(0, 2).start()

    def plane5():
        forward_ring4(3)
        to_sibling(2, 3).start()
        to_sibling(2, 1).start()
        for k in (4, 2):
            end_ring4(k)
            to_sibling(k - 1, 2).start()

    def plane6():
        end_ring4(3)
        to_sibling(2, 2).start()
        for j in range(4):
            for d in range(4):
                to_sibling(j, d).wait_recv()

    def multiply(rows, low, high):
        def one(i, _):
            owner = (z + (i + 1) // 2 * (2 * (i % 2) - 1) + NZ) % NZ
            w = wbuf[pl.ds(owner * 2, 2)].reshape(FEAT, COLS)
            acc[rows, :] += jnp.dot(tok[owner, rows, :], w, preferred_element_type=F32)
            return 0

        if high - low == 1:
            one(low, 0)
        elif high > low:
            lax.fori_loop(low, high, one, 0)

    def kv_copy(ch, d):
        src, dst = (kv.at[key_rows(ch, back), pl.ds(0, 256)] for back in (0, d))
        i = ch * 4 + d - 1
        return copy(src, dst, k_send.at[i], k_recv.at[i], dev((g, (f + d) % 8), z))

    def finish(ch):
        size = SIZES[ch]
        rows = slice(FROM[ch], FROM[ch] + size)
        cosine, sine = trig[0, rows, :], trig[1, rows, :]
        for h in range(4):
            a = acc[rows, HD * h:HD * h + HD]
            queries[h, rows, :] = (a * cosine + pltpu.roll(a, HD // 2, 1) * sine).astype(BF16)
        a = acc[rows, 512:640]
        kv[key_rows(ch, 0), 0:128] = (a * cosine + pltpu.roll(a, HD // 2, 1) * sine).astype(BF16)
        kv[key_rows(ch, 0), 128:256] = acc[rows, 640:768].astype(BF16)
        for d in (4, 3, 2, 1):
            @pl.when(f + d < 8)
            def _():
                kv_copy(ch, d).start()

    def masks(ch):
        size = SIZES[ch]
        n = lax.broadcasted_iota(jnp.int32, (1, (BACK + 1) * size), 1)
        k_at = n + ((f - BACK) * ROWS + FROM[ch])
        for b in range(1, BACK + 1):
            k_at = k_at + jnp.where(n >= b * size, ROWS - size, 0)
        k_at = k_at.astype(F32)
        bias[ch][...] = jnp.where((k_at >= start[:, 0:1]) & (k_at <= row[:, 0:1]), 0.0, -1e30)

    def kv_arrivals(ch):
        for d in range(1, BACK + 1):
            @pl.when(f >= d)
            def _():
                kv_copy(ch, d).wait_recv()

    def attend(j, low, high, heads=range(4)):
        rows = slice(low, high)
        keys = slice((BACK + 1) * FROM[j], (BACK + 1) * (FROM[j] + SIZES[j]))
        for h in heads:
            s = lax.dot_general(queries[h, rows, :], kv[keys, 0:128], (((1,), (1,)), ((), ())), preferred_element_type=F32)
            s = s * (HD ** (-0.5) * LOG2E) + bias[j][rows, :]
            top = jnp.max(s, axis=1, keepdims=True)
            if j > 0:
                before = peak[h, rows, :]
                top = jnp.maximum(before[:, 0:1], top)
            p = jnp.exp2(s - top).astype(BF16)
            o = jnp.dot(p, kv[keys, 128:384], preferred_element_type=F32)
            if j > 0:
                keep = jnp.exp2(before - top)
                o = mixed[h, rows, :] * jnp.concatenate([keep, keep], axis=1) + o
            if j == CHUNKS - 1:
                o_ref[rows, HD * h:HD * h + HD] = (o[:, 0:128] / o[:, 128:256]).astype(BF16)
            else:
                peak[h, rows, :] = jnp.broadcast_to(top, (high - low, HD))
                mixed[h, rows, :] = o

    acc[...] = jnp.zeros((ROWS, COLS), F32)
    then = {
        (0, 0, 1): lambda: masks(0),
        (1, 0, 1): lambda: masks(1),
        (1, 1, 0): lambda: masks(2),
        (0, 2, 1): plane1,
        (2, 1, 1): plane2,
        (3, 1, 1): plane3,
        (4, 1, 1): plane4,
        (5, 1, 1): plane5,
        (6, 1, 1): plane6,
        (10, 1, 1): lambda: (kv_arrivals(0), attend(0, 0, FROM[2], (0, 1))),
        (11, 2, 0): lambda: attend(0, 0, FROM[2], (2,)),
        (11, 2, 1): lambda: attend(0, 0, FROM[2], (3,)),
    }
    weights_in = (6, 2, 0)
    done = [0] * CHUNKS
    have = [0] * CHUNKS
    ended = 0
    for t in range(8 + LAG * (CHUNKS - 1)):
        for ch in sorted(range(CHUNKS), key=lambda ch: t - LAG * ch >= 8):
            step = t - LAG * ch
            if step == 8:
                last_arrivals(ch)
                have[ch] = NZ
            for h in (0, 1):
                if 0 <= step < 8:
                    ring(ch, step, h)
                    if h == 1:
                        have[ch] = 2 * step + 1
                if (t, ch, h) >= weights_in and (0 <= step < 8 or step == 8 and h == 1):
                    for _ in range(2):
                        at = done[ended]
                        if all(done[k] == at and have[k] > at for k in range(ended, CHUNKS)):
                            multiply(slice(FROM[ended], ROWS), at, at + 1)
                            done[ended:] = [at + 1] * (CHUNKS - ended)
                if step == 8 and h == 1:
                    multiply(slice(FROM[ch], FROM[ch] + SIZES[ch]), done[ch], NZ)
                    finish(ch)
                    ended = ch + 1
                then.get((t, ch, h), lambda: None)()
    multiply(slice(FROM[2], ROWS), done[2], NZ - 1)
    last_arrivals(2)
    multiply(slice(FROM[2], ROWS), NZ - 1, NZ)
    finish(2)
    attend(0, FROM[2], ROWS)
    kv_arrivals(1)
    attend(1, 0, ROWS)
    kv_arrivals(2)
    attend(2, 0, ROWS)

    for d in range(1, NZ):
        square(d).wait_send()
        relay(d).wait_send()
    for k in range(5):
        for d in (1, 3):
            near(k, d).wait_send()
            far(k, d).wait_send()
    for j in range(4):
        for d in range(4):
            to_sibling(j, d).wait_send()

    for ch in range(CHUNKS):
        for step in range(8):
            for h, r in WAYS:
                if is_long(h, r) or step < 7:
                    hop(ch, step, h, r).wait_send()
    for ch in range(CHUNKS):
        for d in range(1, BACK + 1):
            @pl.when(f + d < 8)
            def _():
                kv_copy(ch, d).wait_send()


def shards(tokens_in, norm_gain, segment_ids, wq, wk, wv):
    vmem = pl.BlockSpec(memory_space=pltpu.VMEM)
    dma = pltpu.SemaphoreType.DMA
    freqs = 500000.0 ** (-(np.arange(HD) % 64) / 64.0)
    hbm = pl.BlockSpec(memory_space=pl.ANY)
    return pl.pallas_call(
        front,
        name="front",
        out_shape=jax.ShapeDtypeStruct((ROWS, 512), BF16),
        in_specs=[hbm, vmem] + [hbm] * 5,
        out_specs=vmem,
        scratch_shapes=[
            pltpu.VMEM((ROWS, FEAT), BF16),
            pltpu.VMEM((1, 8 * ROWS), jnp.int32),
            pltpu.VMEM((1, HD), F32),
            pltpu.VMEM((16, 8192), F32),
            pltpu.VMEM((16, 1024), F32),
            pltpu.VMEM((16, 1024), F32),
            pltpu.VMEM((NZ, 16, COLS), BF16),
            pltpu.VMEM((32, 256, COLS), BF16),
            pltpu.VMEM((NZ, ROWS, FEAT), BF16),
            pltpu.VMEM((NZ, 1, ROWS), F32),
            pltpu.VMEM((ROWS, COLS), F32),
            pltpu.VMEM((2, ROWS, HD), F32),
            pltpu.VMEM(((BACK + 1) * ROWS, 3 * HD), BF16),
            pltpu.VMEM((4, ROWS, HD), BF16),
            *[pltpu.VMEM((ROWS, (BACK + 1) * size), F32) for size in SIZES],
            pltpu.VMEM((4, ROWS, HD), F32),
            pltpu.VMEM((4, ROWS, 2 * HD), F32),
            dma((6,)),
            dma((NZ,)), dma((NZ,)),
            dma((NZ,)), dma((NZ,)),
            dma((20,)), dma((20,)),
            dma((16,)), dma((16,)),
            dma((2, CHUNKS * 16)), dma((2, CHUNKS * 16)),
            dma((CHUNKS * 4,)), dma((CHUNKS * 4,)),
        ],
        compiler_params=pltpu.CompilerParams(collective_id=1, has_side_effects=True, vmem_limit_bytes=56 << 20),
        cost_estimate=pl.CostEstimate(flops=2 * ROWS * 8192 * COLS, bytes_accessed=4 << 20, transcendentals=0),
    )(tokens_in, norm_gain[None], segment_ids, jnp.asarray(freqs[None], F32), wq, wk, wv)


def solution(mesh):
    placed = (
        P(("group", "fsdp"), "tensor"),
        P("tensor"),
        P("group", None),
        P(("group", "fsdp", "tensor"), None),
        P(("group", "fsdp", "tensor"), None),
        P(("group", "fsdp", "tensor"), None),
    )
    return jax.shard_map(
        shards,
        mesh=mesh,
        in_specs=placed,
        out_specs=P(("group", "fsdp"), "tensor"),
        check_vma=False,
    )
```

time: 151 us -> 127 us (0.84)
  the two profiles are of different devices: /device:TPU:2 before, /device:TPU:36 now
where the time goes in v2:
time: 127 us
  Pallas kernels  124 us (98%)
  local copies, waits for them, and re-layouts  3.03 us (2%)
    pallas_call x1, Pallas kernels, shards(): pl.pallas_call(front, name='front', out_shape=jax.ShapeDtypeStruct((ROWS,...  124 us

profile of v2, /device:TPU:36, one launch (start us, length us, event | category | flops | bytes accessed | tf_op | source)
XLA Modules:
  0.0 126.9 jit_solution(12220576272285168552)
XLA Ops:
  0.0 1.3 broadcast_in_dim.3.gain_ref
  1.3 123.9 %front.1 = bf16[384,512]{1,0:T(8,128)(2,1)} custom-call(bf16[384,512]{1,0:T(8,128)(2,1)} %tok_hbm.1, bf16[1,512]{1,0:T(2,128)(2,1)} %broadcast_in_dim.3.gain_ref, s32[1,3072]{1,0:T(1,128)} %seg_hbm.1, f32[1,128]{1,0:T(1,128)} %constant.2.clone.freq_hbm, f32[16,8192]{1,0:T(8,128)} %wq_hbm.1, f32[16,1024]{1,0:T(8,128)} %wk_hbm.1, f32[16,1024]{1,0:T(8,128)} %wv_hbm.1), custom_call_target="tpu_custom_call" | custom-call | flops 4831838208 | bytes 4194304 | tf_op jit(solution)/shard_map/front/pallas_call | solution.py:398
  125.1 1.8 %copy.9 = bf16[384,512]{1,0:T(8,128)(2,1)} copy(bf16[384,512]{1,0:T(8,128)(2,1)} %front.1) | data formatting | bytes 786432

commit v3 on v2

--- a/solution.py
+++ b/solution.py
@@ -17,9 +17,10 @@
 SIZES = (192, 128, 64)
 CHUNKS = len(SIZES)
 FROM = (0, 192, 320)
-LAG = 2
+START = (0, 2, 3)
 COLS = 768
 BACK = 4
+RELAYED = (0,)
 LOG2E = math.log2(math.e)
 EPS = 1e-05
 
@@ -44,7 +45,7 @@
           wsend, wbuf, tok, ssq, acc, trig, kv, queries, *rest):
     bias = rest[:CHUNKS]
     (peak, mixed, in_sem,
-          a_send, a_recv, s_send, s_recv, p_send, p_recv, b_send, b_recv, r_send, r_recv, k_send, k_recv) = rest[CHUNKS:]
+          a_send, a_recv, s_send, s_recv, p_send, p_recv, b_send, b_recv, r_send, r_recv, k_send, k_recv, r_kv_send) = rest[CHUNKS:]
     g, f, z = lax.axis_index("group"), lax.axis_index("fsdp"), lax.axis_index("tensor")
     x, y, c = f // 2, (f % 2) * 2 + g // 2, g % 2
 
@@ -66,9 +67,6 @@
             (tok_hbm, tok_ref), (wq_hbm, wq_ref), (wk_hbm, wk_ref), (wv_hbm, wv_ref),
             (seg_hbm, seg_ref), (freq_hbm, freq_ref)))
     ]
-    for load in loads:
-        load.start()
-
     bar = pltpu.get_barrier_semaphore()
     count = 0
     for d in range(1, NZ):
@@ -85,6 +83,9 @@
         pl.semaphore_signal(bar, inc=1, device_id=dev((g, (f + d) % 8), z), device_id_type=MESH)
         count += 1
 
+    for load in loads:
+        load.start()
+
     loads[0].wait()
     floats = tok_ref[...].astype(F32)
     part = jnp.sum(floats * floats, axis=1, keepdims=True)
@@ -140,7 +141,7 @@
     scale = lax.rsqrt(jnp.broadcast_to(total, (128, ROWS)).T * (1.0 / 8192) + EPS)
     for j in range(FEAT // 128):
         cut = slice(128 * j, 128 * j + 128)
-        tok[z, :, cut] = (tok_ref[:, cut].astype(F32) * scale * gain_ref[:, cut].astype(F32)).astype(BF16)
+        tok[z, :, cut] = (tok_ref[:, cut].astype(F32) * scale * gain_ref[cut].astype(F32)[None]).astype(BF16)
 
     def hop(ch, step, h, r):
         to = (z + 1 - 2 * r + NZ) % NZ
@@ -264,6 +265,18 @@
         src, dst = (kv.at[key_rows(ch, back), pl.ds(0, 256)] for back in (0, d))
         i = ch * 4 + d - 1
         return copy(src, dst, k_send.at[i], k_recv.at[i], dev((g, (f + d) % 8), z))
+
+    def kv_relay(ch, d):
+        at = d + 1 - 2 * (f % 2)
+        src = kv.at[key_rows(ch, d), pl.ds(0, 256)]
+        dst = kv.at[pl.ds(pl.multiple_of((BACK + 1) * FROM[ch] + (BACK - at) * SIZES[ch], 32), SIZES[ch]), pl.ds(0, 256)]
+        return copy(src, dst, r_kv_send.at[ch * 2 + d // 2 - 1], k_recv.at[ch * 4 + at - 1], dev((g, f + 1 - 2 * (f % 2)), z))
+
+    def relays(ch, d):
+        @pl.when((f >= d) & (f % 2 >= d // 4))
+        def _():
+            kv_copy(ch, d).wait_recv()
+            kv_relay(ch, d).start()
 
     def finish(ch):
         size = SIZES[ch]
@@ -275,10 +288,20 @@
         a = acc[rows, 512:640]
         kv[key_rows(ch, 0), 0:128] = (a * cosine + pltpu.roll(a, HD // 2, 1) * sine).astype(BF16)
         kv[key_rows(ch, 0), 128:256] = acc[rows, 640:768].astype(BF16)
-        for d in (4, 3, 2, 1):
-            @pl.when(f + d < 8)
+        if ch in RELAYED:
+            for d in (4, 2):
+                @pl.when(f + d < 8)
+                def _():
+                    kv_copy(ch, d).start()
+
+            @pl.when(f % 2 == 0)
             def _():
-                kv_copy(ch, d).start()
+                kv_copy(ch, 1).start()
+        else:
+            for d in (4, 3, 2, 1):
+                @pl.when(f + d < 8)
+                def _():
+                    kv_copy(ch, d).start()
 
     def masks(ch):
         size = SIZES[ch]
@@ -291,7 +314,9 @@
 
     def kv_arrivals(ch):
         for d in range(1, BACK + 1):
-            @pl.when(f >= d)
+            taken = {2: 0, 4: 1}.get(d, 2) if ch in RELAYED else 2
+
+            @pl.when((f >= d) & (f % 2 < taken))
             def _():
                 kv_copy(ch, d).wait_recv()
 
@@ -327,17 +352,16 @@
         (4, 1, 1): plane4,
         (5, 1, 1): plane5,
         (6, 1, 1): plane6,
-        (10, 1, 1): lambda: (kv_arrivals(0), attend(0, 0, FROM[2], (0, 1))),
-        (11, 2, 0): lambda: attend(0, 0, FROM[2], (2,)),
-        (11, 2, 1): lambda: attend(0, 0, FROM[2], (3,)),
+        (9, 2, 1): lambda: relays(0, 2),
+        (10, 1, 1): lambda: relays(0, 4),
     }
     weights_in = (6, 2, 0)
     done = [0] * CHUNKS
     have = [0] * CHUNKS
     ended = 0
-    for t in range(8 + LAG * (CHUNKS - 1)):
-        for ch in sorted(range(CHUNKS), key=lambda ch: t - LAG * ch >= 8):
-            step = t - LAG * ch
+    for t in range(8 + START[-1]):
+        for ch in sorted(range(CHUNKS), key=lambda ch: t - START[ch] >= 8):
+            step = t - START[ch]
             if step == 8:
                 last_arrivals(ch)
                 have[ch] = NZ
@@ -361,7 +385,8 @@
     last_arrivals(2)
     multiply(slice(FROM[2], ROWS), NZ - 1, NZ)
     finish(2)
-    attend(0, FROM[2], ROWS)
+    kv_arrivals(0)
+    attend(0, 0, ROWS)
     kv_arrivals(1)
     attend(1, 0, ROWS)
     kv_arrivals(2)
@@ -384,10 +409,28 @@
                 if is_long(h, r) or step < 7:
                     hop(ch, step, h, r).wait_send()
     for ch in range(CHUNKS):
-        for d in range(1, BACK + 1):
-            @pl.when(f + d < 8)
+        if ch in RELAYED:
+            for d in (2, 4):
+                @pl.when(f + d < 8)
+                def _():
+                    kv_copy(ch, d).wait_send()
+
+                @pl.when((f >= d) & (f % 2 >= d // 4))
+                def _():
+                    kv_relay(ch, d).wait_send()
+
+            @pl.when(f % 2 == 0)
             def _():
-                kv_copy(ch, d).wait_send()
+                kv_copy(ch, 1).wait_send()
+        else:
+            for d in range(1, BACK + 1):
+                @pl.when(f + d < 8)
+                def _():
+                    kv_copy(ch, d).wait_send()
+
+
+def hand_over(in_ref, out_ref):
+    out_ref[...] = in_ref[...]
 
 
 def shards(tokens_in, norm_gain, segment_ids, wq, wk, wv):
@@ -395,7 +438,7 @@
     dma = pltpu.SemaphoreType.DMA
     freqs = 500000.0 ** (-(np.arange(HD) % 64) / 64.0)
     hbm = pl.BlockSpec(memory_space=pl.ANY)
-    return pl.pallas_call(
+    attended = pl.pallas_call(
         front,
         name="front",
         out_shape=jax.ShapeDtypeStruct((ROWS, 512), BF16),
@@ -425,11 +468,18 @@
             dma((20,)), dma((20,)),
             dma((16,)), dma((16,)),
             dma((2, CHUNKS * 16)), dma((2, CHUNKS * 16)),
-            dma((CHUNKS * 4,)), dma((CHUNKS * 4,)),
+            dma((CHUNKS * 4,)), dma((CHUNKS * 4,)), dma((CHUNKS * 2,)),
         ],
         compiler_params=pltpu.CompilerParams(collective_id=1, has_side_effects=True, vmem_limit_bytes=56 << 20),
         cost_estimate=pl.CostEstimate(flops=2 * ROWS * 8192 * COLS, bytes_accessed=4 << 20, transcendentals=0),
-    )(tokens_in, norm_gain[None], segment_ids, jnp.asarray(freqs[None], F32), wq, wk, wv)
+    )(tokens_in, norm_gain, segment_ids, jnp.asarray(freqs[None], F32), wq, wk, wv)
+    return pl.pallas_call(
+        hand_over,
+        name="hand_over",
+        out_shape=jax.ShapeDtypeStruct((ROWS, 512), BF16),
+        in_specs=[vmem],
+        out_specs=vmem,
+    )(attended)
 
 
 def solution(mesh):

time: 127 us -> 121 us (0.953)
  local copies, waits for them, and re-layouts: 3.03 us -> 0 us
  Pallas kernels: 124 us -> 121 us
    pallas_call x1, Pallas kernels: 124 us -> 119 us  [shards(): pl.pallas_call(front, name='front', out_shape=jax.ShapeDtypeStruct((ROWS,...]
    pallas_call x0 -> x1, Pallas kernels: none -> 1.77 us  [shards(): pl.pallas_call(hand_over, name='hand_over', out_shape=jax.ShapeDtypeStruc...]
    unnamed x1 -> x0, local copies, waits for them, and re-layouts: 1.77 us -> none
where the time goes in v3:
time: 121 us
  Pallas kernels  121 us (100%)
    pallas_call x1, Pallas kernels, shards(): pl.pallas_call(front, name='front', out_shape=jax.ShapeDtypeStruct((ROWS,...  119 us

profile of v3, /device:TPU:36, one launch (start us, length us, event | category | flops | bytes accessed | tf_op | source)
XLA Modules:
  0.0 121.1 jit_solution(8400168296333596489)
XLA Ops:
  0.0 119.4 %front.1.in_ref = bf16[384,512]{1,0:T(8,128)(2,1)} custom-call(bf16[384,512]{1,0:T(8,128)(2,1)} %tok_hbm.1, bf16[512]{0:T(512)(128)(2,1)} %gain_ref.1, s32[1,3072]{1,0:T(1,128)} %seg_hbm.1, f32[1,128]{1,0:T(1,128)} %constant.2.clone.freq_hbm, f32[16,8192]{1,0:T(8,128)} %wq_hbm.1, f32[16,1024]{1,0:T(8,128)} %wk_hbm.1, f32[16,1024]{1,0:T(8,128)} %wv_hbm.1), custom_call_target="tpu_custom_call" | custom-call | flops 4831838208 | bytes 4194304 | tf_op jit(solution)/shard_map/front/pallas_call | solution.py:441
  119.4 1.8 %hand_over.1 = bf16[384,512]{1,0:T(8,128)(2,1)} custom-call(bf16[384,512]{1,0:T(8,128)(2,1)} %front.1.in_ref), custom_call_target="tpu_custom_call" | custom-call | tf_op jit(solution)/shard_map/hand_over/pallas_call | solution.py:476

commit v4 on v3

--- a/solution.py
+++ b/solution.py
@@ -320,12 +320,13 @@
             def _():
                 kv_copy(ch, d).wait_recv()
 
-    def attend(j, low, high, heads=range(4)):
+    def attend(j, low, high, heads=range(4), skip=0):
         rows = slice(low, high)
-        keys = slice((BACK + 1) * FROM[j], (BACK + 1) * (FROM[j] + SIZES[j]))
+        width = (BACK + 1) * SIZES[j] - skip
+        keys = slice((BACK + 1) * FROM[j], (BACK + 1) * FROM[j] + width)
         for h in heads:
             s = lax.dot_general(queries[h, rows, :], kv[keys, 0:128], (((1,), (1,)), ((), ())), preferred_element_type=F32)
-            s = s * (HD ** (-0.5) * LOG2E) + bias[j][rows, :]
+            s = s * (HD ** (-0.5) * LOG2E) + bias[j][rows, 0:width]
             top = jnp.max(s, axis=1, keepdims=True)
             if j > 0:
                 before = peak[h, rows, :]
@@ -390,7 +391,8 @@
     kv_arrivals(1)
     attend(1, 0, ROWS)
     kv_arrivals(2)
-    attend(2, 0, ROWS)
+    attend(2, 0, FROM[2], skip=SIZES[2])
+    attend(2, FROM[2], ROWS)
 
     for d in range(1, NZ):
         square(d).wait_send()

time: 121 us -> 121 us (level)
  no operation moved by 1% of the time
where the time goes in v4:
time: 121 us
  Pallas kernels  121 us (100%)
    pallas_call x1, Pallas kernels, shards(): pl.pallas_call(front, name='front', out_shape=jax.ShapeDtypeStruct((ROWS,...  119 us

profile of v4, /device:TPU:36, one launch (start us, length us, event | category | flops | bytes accessed | tf_op | source)
XLA Modules:
  0.0 121.1 jit_solution(13093951015982858007)
XLA Ops:
  0.0 119.3 %front.1.in_ref = bf16[384,512]{1,0:T(8,128)(2,1)} custom-call(bf16[384,512]{1,0:T(8,128)(2,1)} %tok_hbm.1, bf16[512]{0:T(512)(128)(2,1)} %gain_ref.1, s32[1,3072]{1,0:T(1,128)} %seg_hbm.1, f32[1,128]{1,0:T(1,128)} %constant.2.clone.freq_hbm, f32[16,8192]{1,0:T(8,128)} %wq_hbm.1, f32[16,1024]{1,0:T(8,128)} %wk_hbm.1, f32[16,1024]{1,0:T(8,128)} %wv_hbm.1), custom_call_target="tpu_custom_call" | custom-call | flops 4831838208 | bytes 4194304 | tf_op jit(solution)/shard_map/front/pallas_call | solution.py:443
  119.3 1.8 %hand_over.1 = bf16[384,512]{1,0:T(8,128)(2,1)} custom-call(bf16[384,512]{1,0:T(8,128)(2,1)} %front.1.in_ref), custom_call_target="tpu_custom_call" | custom-call | tf_op jit(solution)/shard_map/hand_over/pallas_call | solution.py:478
